TPU v7x, 32 devices: a whole 2x2x4 slice. The times are simulated.
32 devices in a mesh: shard: 4 (over z), dp: 8 (over y, x, core).
Axes of the slice: x: 2, y: 2, z: 4, core: 2. Of those that a mesh axis runs over, the one named last changes fastest.
Arguments:
- cache_state: float32 [8, 4, 64, 384], P('dp', 'shard'), as said below
- table_state: float32 [8, 4, 128, 384], P('dp', 'shard'), as said below
- batch_idx: int32 [8, 4, 1024, 8], P('dp', 'shard'), may hold values from 0 to 63
- loss_grad: float32 [8, 4, 1024], P('dp', 'shard'), may hold values from -6 to 6
- w_first: bfloat16 [1024, 1024], replicated, may hold values from -0.1875 to 0.1875
- head: float32 [1024], replicated, may hold values from -6 to 6
- home: int32 [8, 512], P('dp'), may hold values from 0 to 511, as said below
- fetch_rows: int32 [8, 4, 4, 16], P('dp', 'shard'), may hold values from 0 to 511, as said below
- fetch_counts: int32 [8, 4, 4], P('dp', 'shard'), may hold values from 0 to 16, as said below
- evict_rows: int32 [8, 4, 4, 16], P('dp', 'shard'), may hold values from 0 to 511, as said below
- evict_from: int32 [8, 4, 4, 16], P('dp', 'shard'), may hold values from 0 to 63, as said below
- evict_counts: int32 [8, 4, 4], P('dp', 'shard'), may hold values from 0 to 16, as said below
Outputs:
- grad_first: bfloat16 [1024, 1024], P('shard')
- table_after: float32 [8, 4, 128, 384], P('dp', 'shard')
- fetched: float32 [8, 4, 4, 16, 384], P('dp', 'shard')
Inputs may be any that keep to these rules, and one draw needn't show every extreme that they name: In each group home is a permutation; row r belongs to owner home[r] // 128. `fetch_rows`: every entry, live or not, names a row of the owner whose list it is in; no row is live both in a fetch list and in a write-back list of the same group. `fetch_counts`: in every group some owner gets 16 from every device. `evict_rows`: every entry names a row of the owner whose list it is in; live entries of a group are all different rows. `evict_from`: the entries of one device are all different. `evict_counts`: in every group some owner gets 16 from every device. `cache_state`: the last 128 entries of a row are positive. `table_state`: the last 128 entries of a row are positive.
All inputs are finite; a program needn't handle non-finite values.
Results may differ from a plain program's by a relative error of at most 0.0061.
Values sent between devices are 32-bit elements; how exact they have to be, the bound alone decides.
A program may use at most 64 MiB of HBM per device.

v0:
```python
import math

import jax
import jax.numpy as jnp
from jax import lax
from jax.sharding import PartitionSpec as P

beta_one = 0.9
beta_two = 0.999
learn_rate = 0.05
epsilon = 1e-08
bias_one = 1.0 - 0.9**10
bias_two = 1.0 - 0.999**10


def adam_rows(state, grads, embed):
    value = state[:, :embed]
    first = state[:, embed : 2 * embed]
    second = state[:, 2 * embed :]
    first = beta_one * first + (1.0 - beta_one) * grads
    second = beta_two * second + (1.0 - beta_two) * grads * grads
    value = value - learn_rate * (first / bias_one) / (jnp.sqrt(second / bias_two) + epsilon)
    return jnp.concatenate([value, first, second], axis=1)


def local(
    cache_state,
    table_state,
    batch_idx,
    loss_grad,
    w_first,
    head,
    home,
    fetch_rows,
    fetch_counts,
    evict_rows,
    evict_from,
    evict_counts,
):
    group = lax.axis_size("shard")
    cache = cache_state[0, 0]
    table = table_state[0, 0]
    batch = batch_idx[0, 0]
    loss = loss_grad[0, 0]
    home_map = home[0]
    wanted = fetch_rows[0, 0]
    gone = evict_rows[0, 0]
    gone_from = evict_from[0, 0]
    width = cache.shape[1]
    embed = width // 3
    table_rows = table.shape[0]
    cache_rows = cache.shape[0]
    capacity = wanted.shape[1]
    mlp_width = w_first.shape[0]
    samples = batch.shape[0]
    within = jnp.arange(capacity, dtype=jnp.int32)[None, :]
    wanted_live = within < fetch_counts[0, 0][:, None]
    gone_live = within < evict_counts[0, 0][:, None]
    place = (
        jnp.take(
            home_map,
            lax.all_to_all(wanted, "shard", split_axis=0, concat_axis=0, tiled=True),
            axis=0,
        )
        % table_rows
    )
    arrived = lax.all_to_all(
        jnp.take(table, place, axis=0), "shard", split_axis=0, concat_axis=0, tiled=True
    )
    flat_batch = batch.reshape(-1)
    looked = jnp.take(cache[:, :embed], flat_batch, axis=0)
    inputs = looked.reshape(samples, mlp_width).astype(jnp.bfloat16)
    pre = jnp.dot(inputs, w_first, preferred_element_type=jnp.float32)
    sigma = jax.nn.sigmoid(pre)
    delta = (loss[:, None] * head[None, :] * sigma * (1.0 + pre * (1.0 - sigma))).astype(
        jnp.bfloat16
    )
    back = lax.dot_general(
        delta, w_first, (((1,), (1,)), ((), ())), preferred_element_type=jnp.float32
    )
    positions = jnp.arange(cache_rows, dtype=jnp.int32)
    onehot = (flat_batch[:, None] == positions[None, :]).astype(jnp.float32)
    grads = lax.dot_general(
        onehot,
        back.reshape(-1, embed),
        (((0,), (0,)), ((), ())),
        precision=lax.Precision.HIGHEST,
        preferred_element_type=jnp.float32,
    )
    updated = adam_rows(cache, grads, embed)
    sent_rows = jnp.take(updated, gone_from.reshape(-1), axis=0).reshape(group, capacity, width)
    sent_slots = jnp.where(gone_live, jnp.take(home_map, gone, axis=0) % table_rows, table_rows)
    got_rows, got_slots = (
        lax.all_to_all(sent_rows, "shard", split_axis=0, concat_axis=0, tiled=True),
        lax.all_to_all(sent_slots, "shard", split_axis=0, concat_axis=0, tiled=True),
    )
    new_table = table.at[got_slots.reshape(-1)].set(got_rows.reshape(-1, width), mode="drop")
    fetched = jnp.where(wanted_live[:, :, None], arrived, jnp.zeros_like(arrived))
    scale = 1.0 / math.sqrt(samples * group * lax.axis_size("dp"))
    partial_rows = lax.psum_scatter(
        lax.dot_general(
            inputs, delta, (((0,), (0,)), ((), ())), preferred_element_type=jnp.float32
        ),
        "shard",
        scatter_dimension=0,
        tiled=True,
    )
    mine = lax.psum(partial_rows, "dp")
    grad_first = (mine * scale).astype(jnp.bfloat16)
    return (grad_first, new_table[None, None], fetched[None, None])


def solution(mesh):
    placed = (
        P("dp", "shard", None, None),
        P("dp", "shard", None, None),
        P("dp", "shard", None, None),
        P("dp", "shard", None),
        P(),
        P(),
        P("dp", None),
        P("dp", "shard", None, None),
        P("dp", "shard", None),
        P("dp", "shard", None, None),
        P("dp", "shard", None, None),
        P("dp", "shard", None),
    )
    return jax.shard_map(
        local,
        mesh=mesh,
        in_specs=placed,
        out_specs=(
            P("shard", None),
            P("dp", "shard", None, None),
            P("dp", "shard", None, None, None),
        ),
        check_vma=False,
    )
```

profile of v0, /device:TPU:1, one launch (start us, length us, event | category | flops | bytes accessed | tf_op | source)
XLA Modules:
  0.0 206.7 jit_solution(3958130132201150747)
XLA Ops:
  7.2 1.1 copy.38
  8.3 0.8 compare_and_fusion
  9.1 1.0 copy.25
  11.4 29.4 %gather_fusion = bf16[8192,128]{1,0:T(8,128)(2,1)} fusion(bf16[64,128]{1,0:T(8,128)(2,1)S(1)} %slice.23, s32[8192]{0:T(1024)S(1)} %broadcast_clamp_fusion), kind=kCustom, calls=%fused_computation.2 | custom fusion | bytes 4227072 | tf_op jit(solution)/shard_map/jit(_take)/gather | solution.py:71
  40.8 4.2 %gather.20 = bf16[1024,1024]{1,0:T(8,128)(2,1)} reshape(bf16[8192,128]{1,0:T(8,128)(2,1)} %gather_fusion) | data formatting | bytes 4194304 | tf_op jit(solution)/shard_map/jit(_take)/gather | solution.py:71
  45.0 3.2 %broadcast_in_dim.62 = pred[1024,8,128]{2,1,0:T(8,128)(4,1)S(1)} broadcast(pred[1024,8]{1,0:T(8,128)(4,1)S(1)} %copy.24), dimensions={0,1} | broadcast | bytes 1056768 | tf_op jit(solution)/shard_map/jit(_take)/broadcast_in_dim | solution.py:71
  48.2 5.1 %multiply_convert_fusion = bf16[1024,1024]{1,0:T(8,128)(2,1)S(1)} fusion(f32[1024]{0:T(1024)S(1)} %copy-done.7, f32[1024]{0:T(1024)S(1)} %bitcast.69, bf16[1024,1024]{1,0:T(8,128)(2,1)S(1)} %copy-done, bf16[1024,1024]{1,0:T(8,128)(2,1)} %gather.20, pred[128,8,8,128]{3,2,1,0:T(8,128)(4,1)S(1)} %bitcast.58), kind=kOutput, calls=%fused_computation.6 | convolution fusion | flops 2159017984 | bytes 7348224 | tf_op jit(solution)/shard_map/dot_general | solution.py:73
  53.3 1.4 copy-done.10
  54.7 4.5 %fusion.4 = f32[1024,1024]{1,0:T(8,128)} fusion(bf16[1024,1024]{1,0:T(8,128)(2,1)S(1)} %multiply_convert_fusion, bf16[1024,1024]{1,0:T(8,128)(2,1)S(1)} %copy-done.3, pred[128,8,8,128]{3,2,1,0:T(8,128)(4,1)S(1)} %bitcast.59), kind=kOutput, calls=%fused_computation.25 | convolution fusion | flops 2148532224 | bytes 9437184 | tf_op jit(solution)/shard_map/dot_general | solution.py:101
  59.1 5.6 %all-to-all-start.2 = ((s32[4,1,16]{2,1,0:T(1,128)}), s32[4,1,16]{2,1,0:T(1,128)S(1)}, u32[]{:S(2)}, u32[]{:S(2)}) async-start(s32[4,1,16]{2,1,0:T(1,128)} %bitcast.18), calls=%async_computation.3 | async-start | bytes 4096 | tf_op jit(solution)/shard_map/all_to_all | solution.py:62
  65.2 0.8 gather_fusion.3
  66.0 5.9 %fusion.15 = f32[1024,1024]{1,0:T(8,128)} fusion(bf16[1024,1024]{1,0:T(8,128)(2,1)} %copy-done.10, bf16[1024,1024]{1,0:T(8,128)(2,1)S(1)} %copy-done), kind=kOutput, calls=%fused_computation.55 | convolution fusion | flops 2147483648 | bytes 8388608 | tf_op jit(solution)/shard_map/dot_general | solution.py:78
  72.0 4.9 %reshape.168 = f32[8192,128]{1,0:T(8,128)} reshape(f32[1024,1024]{1,0:T(8,128)} %fusion.15) | data formatting | bytes 8388608 | tf_op jit(solution)/shard_map/reshape | solution.py:85
  76.9 4.1 %divide_subtract_fusion = (f32[64,128]{1,0:T(8,128)S(1)}, f32[64,128]{1,0:T(8,128)S(1)}, f32[64,128]{1,0:T(8,128)S(1)}) fusion(f32[64,384]{1,0:T(8,128)} %bitcast.65, f32[8192,128]{1,0:T(8,128)} %reshape.168, s32[8192]{0:T(1024)S(1)} %reshape_squeeze.15), kind=kOutput, calls=%fused_computation.23 | convolution fusion | flops 805928960 | bytes 4423680 | tf_op jit(solution)/shard_map/dot_general | solution.py:83
  83.2 4.6 %all-to-all-start = ((s32[4,1,16]{2,1,0:T(1,128)}), s32[4,1,16]{2,1,0:T(1,128)S(1)}, u32[]{:S(2)}, u32[]{:S(2)}) async-start(s32[4,1,16]{2,1,0:T(1,128)} %bitcast.9), calls=%async_computation.1 | async-start | bytes 4096 | tf_op jit(solution)/shard_map/all_to_all | solution.py:95
  87.9 0.8 gather_fusion.4
  89.6 48.8 %reduce-scatter.2.cloned.1.call-done = f32[256,1024]{1,0:T(8,128)} async-done(((f32[1024,1024]{1,0:T(8,128)}), f32[256,1024]{1,0:T(8,128)}) %reduce-scatter.2.cloned.1.call-update) | async-done | bytes 1048592 | tf_op jit(solution)/shard_map/reduce_scatter | solution.py:100
  138.3 3.9 %all-to-all-start.1 = ((f32[4,16,384]{2,1,0:T(8,128)}), f32[4,16,384]{2,1,0:T(8,128)S(1)}, u32[]{:S(2)}, u32[]{:S(2)}) async-start(f32[4,16,384]{2,1,0:T(8,128)} %broadcast_select_fusion.1), calls=%async_computation.2 | async-start | bytes 196608 | tf_op jit(solution)/shard_map/all_to_all | solution.py:94
  144.2 2.7 %all-to-all-done.1 = f32[4,16,384]{2,1,0:T(8,128)S(1)} async-done(((f32[4,16,384]{2,1,0:T(8,128)}), f32[4,16,384]{2,1,0:T(8,128)S(1)}, u32[]{:S(2)}, u32[]{:S(2)}) %all-to-all-start.1) | async-done | bytes 98336 | tf_op jit(solution)/shard_map/all_to_all | solution.py:94
  146.9 3.3 %all-to-all-start.3 = ((f32[4,16,384]{2,1,0:T(8,128)}), f32[4,16,384]{2,1,0:T(8,128)S(1)}, u32[]{:S(2)}, u32[]{:S(2)}) async-start(f32[4,16,384]{2,1,0:T(8,128)} %broadcast_select_fusion), calls=%async_computation.4 | async-start | bytes 196608 | tf_op jit(solution)/shard_map/all_to_all | solution.py:67
  150.2 0.9 scatter_fusion
  151.2 3.7 %all-to-all-done.3 = f32[4,16,384]{2,1,0:T(8,128)S(1)} async-done(((f32[4,16,384]{2,1,0:T(8,128)}), f32[4,16,384]{2,1,0:T(8,128)S(1)}, u32[]{:S(2)}, u32[]{:S(2)}) %all-to-all-start.3) | async-done | bytes 98336 | tf_op jit(solution)/shard_map/all_to_all | solution.py:67
  155.6 42.2 %all-reduce.2.cloned.1.call-done = f32[256,1024]{1,0:T(8,128)} async-done(((f32[256,1024]{1,0:T(8,128)}), f32[256,1024]{1,0:T(8,128)}) %all-reduce.2.cloned.1.call-update) | async-done | bytes 1048592 | tf_op jit(solution)/shard_map/psum | solution.py:108
  197.8 2.1 %multiply_convert_fusion.1 = bf16[256,1024]{1,0:T(8,128)(2,1)} fusion(f32[256,1024]{1,0:T(8,128)} %all-reduce.2.cloned.1.call-done), kind=kLoop, calls=%fused_computation.11 | loop fusion | flops 524288 | bytes 1572864 | tf_op jit(solution)/shard_map/convert_element_type | solution.py:109
  (60 shorter events, 7.8 us)
Async XLA Ops:
  7.2 41.0 %copy-start = (bf16[1024,1024]{1,0:T(8,128)(2,1)S(1)}, bf16[1024,1024]{1,0:T(8,128)(2,1)}, u32[]{:S(2)}) copy-start(bf16[1024,1024]{1,0:T(8,128)(2,1)} %param.18) | copy-start | bytes 6291460
  7.2 131.1 %reduce-scatter.2.cloned.1.call-start = ((), (), s32[]{:S(2)}) async-start(), calls=%async_computation.5 | async-start | bytes 5242880 | tf_op jit(solution)/shard_map/reduce_scatter | solution.py:100
  40.8 7.4 %copy-start.7 = (f32[1024]{0:T(1024)S(1)}, f32[1024]{0:T(1024)}, u32[]{:S(2)}) copy-start(f32[1024]{0:T(1024)} %param.19) | copy-start | bytes 12292
  40.8 7.4 %copy-start.8 = (f32[1,1,1024]{2,1,0:T(1,128)S(1)}, f32[1,1,1024]{2,1,0:T(1,128)}, u32[]{:S(2)}) copy-start(f32[1,1,1024]{2,1,0:T(1,128)} %param.17) | copy-start | bytes 12292
  48.2 6.5 %copy-start.3 = (bf16[1024,1024]{1,0:T(8,128)(2,1)S(1)}, bf16[1024,1024]{1,0:T(8,128)(2,1)}, u32[]{:S(2)}) copy-start(bf16[1024,1024]{1,0:T(8,128)(2,1)} %gather.20) | copy-start | bytes 6291460
  53.3 1.4 copy-start.10
  59.1 5.8 %copy-start.4 = (s32[1,1,4,16]{3,2,1,0:T(4,128)S(1)}, s32[1,1,4,16]{3,2,1,0:T(4,128)}, u32[]{:S(2)}) copy-start(s32[1,1,4,16]{3,2,1,0:T(4,128)} %param.24) | copy-start | bytes 772
  59.1 5.9 %copy-start.5 = (s32[1,1,4,16]{3,2,1,0:T(4,128)S(1)}, s32[1,1,4,16]{3,2,1,0:T(4,128)}, u32[]{:S(2)}) copy-start(s32[1,1,4,16]{3,2,1,0:T(4,128)} %param.23) | copy-start | bytes 772
  59.1 6.0 %copy-start.1 = (s32[1,512]{1,0:T(1,128)S(1)}, s32[1,512]{1,0:T(1,128)}, u32[]{:S(2)}) copy-start(s32[1,512]{1,0:T(1,128)} %param.20) | copy-start | bytes 6148
  59.1 24.1 %all-to-all-start.2 = ((s32[4,1,16]{2,1,0:T(1,128)}), s32[4,1,16]{2,1,0:T(1,128)S(1)}, u32[]{:S(2)}, u32[]{:S(2)}) async-start(s32[4,1,16]{2,1,0:T(1,128)} %bitcast.18), calls=%async_computation.3 | async-start | bytes 4096 | tf_op jit(solution)/shard_map/all_to_all | solution.py:62
  76.9 4.9 %copy-start.6 = (s32[1,1,4]{2,1,0:T(1,128)S(1)}, s32[1,1,4]{2,1,0:T(1,128)}, u32[]{:S(2)}) copy-start(s32[1,1,4]{2,1,0:T(1,128)} %param.25) | copy-start | bytes 52
  76.9 6.2 %copy-start.9 = (s32[1,1,4]{2,1,0:T(1,128)S(1)}, s32[1,1,4]{2,1,0:T(1,128)}, u32[]{:S(2)}) copy-start(s32[1,1,4]{2,1,0:T(1,128)} %param.22) | copy-start | bytes 52
  83.2 55.1 %all-to-all-start = ((s32[4,1,16]{2,1,0:T(1,128)}), s32[4,1,16]{2,1,0:T(1,128)S(1)}, u32[]{:S(2)}, u32[]{:S(2)}) async-start(s32[4,1,16]{2,1,0:T(1,128)} %bitcast.9), calls=%async_computation.1 | async-start | bytes 4096 | tf_op jit(solution)/shard_map/all_to_all | solution.py:95
  87.8 110.0 %all-reduce.2.cloned.1.call-start = ((), (), s32[]{:S(2)}) async-start(), calls=%async_computation.6 | async-start | bytes 2097152 | tf_op jit(solution)/shard_map/psum | solution.py:108
  138.3 8.5 %all-to-all-start.1 = ((f32[4,16,384]{2,1,0:T(8,128)}), f32[4,16,384]{2,1,0:T(8,128)S(1)}, u32[]{:S(2)}, u32[]{:S(2)}) async-start(f32[4,16,384]{2,1,0:T(8,128)} %broadcast_select_fusion.1), calls=%async_computation.2 | async-start | bytes 196608 | tf_op jit(solution)/shard_map/all_to_all | solution.py:94
  146.9 8.0 %all-to-all-start.3 = ((f32[4,16,384]{2,1,0:T(8,128)}), f32[4,16,384]{2,1,0:T(8,128)S(1)}, u32[]{:S(2)}, u32[]{:S(2)}) async-start(f32[4,16,384]{2,1,0:T(8,128)} %broadcast_select_fusion), calls=%async_computation.4 | async-start | bytes 196608 | tf_op jit(solution)/shard_map/all_to_all | solution.py:67
  151.1 48.8 %copy-start.2 = (f32[128,384]{1,0:T(8,128)}, f32[128,384]{1,0:T(8,128)S(1)}, u32[]{:S(2)}) copy-start(f32[128,384]{1,0:T(8,128)S(1)} %scatter_fusion) | copy-start | bytes 589828
Sparse Core Ops, SparseCore 0:
  59.3 78.9 reduce-scatter.1
  141.8 55.9 all-reduce.1
where the time goes:
time: 209 us; the launch traced here: 207 us
  waiting for transfers between devices  97.4 us (47%)
  local copies, waits for them, and re-layouts  51.6 us (25%)
  matrix products  19.6 us (9%)
  starting transfers between devices  17.3 us (8%)
  between operations  14.3 us (7%)
  other arithmetic  6.55 us (3%)
    reduce_scatter x1, waiting for transfers between devices, local(): lax.psum_scatter(lax.dot_general(inputs, delta, (((0,), (0,)), ((), ())),...  48.8 us
    psum x1, waiting for transfers between devices, local(): mine = lax.psum(partial_rows, 'dp')  42.2 us
    gather x2, local copies, waits for them, and re-layouts, local(): looked = jnp.take(cache[:, :embed], flat_batch, axis=0)  33.6 us
    dot_general x1, matrix products, local(): lax.dot_general(delta, w_first, (((1,), (1,)), ((), ())), preferred_eleme...  5.95 us
    all_to_all x1, starting transfers between devices, local(): lax.all_to_all(wanted, 'shard', split_axis=0, concat_axis=0, tiled=True)  5.57 us
    dot_general x1, matrix products, local(): pre = jnp.dot(inputs, w_first, preferred_element_type=jnp.float32)  5.07 us
    reshape x1, local copies, waits for them, and re-layouts, local(): back.reshape(-1, embed)  4.92 us
    all_to_all x1, starting transfers between devices, local(): lax.all_to_all(sent_slots, 'shard', split_axis=0, concat_axis=0, tiled=True)  4.56 us
  transfers between devices with their start and end apart: 6, of which 4 were waited for; matrix products, arithmetic and copies ran while one was open for 12% of the time, Pallas kernels for 0%

commit v1 on v0

--- a/solution.py
+++ b/solution.py
@@ -1,8 +1,11 @@
+import functools
 import math
 
 import jax
 import jax.numpy as jnp
 from jax import lax
+from jax.experimental import pallas as pl
+from jax.experimental.pallas import tpu as pltpu
 from jax.sharding import PartitionSpec as P
 
 beta_one = 0.9
@@ -110,6 +113,398 @@
     return (grad_first, new_table[None, None], fetched[None, None])
 
 
+CHUNK = 256
+PIECE = 16
+BF = jnp.bfloat16
+F32 = jnp.float32
+EXACT = lax.Precision.HIGHEST
+
+
+def dot(a, b, dims, precision=None):
+    return lax.dot_general(
+        a, b, (dims, ((), ())), precision=precision, preferred_element_type=F32
+    )
+
+
+NN = ((1,), (0,))
+NT = ((1,), (1,))
+TN = ((0,), (0,))
+
+
+def split_two(a):
+    high = a.astype(BF)
+    return high, (a - high.astype(F32)).astype(BF)
+
+
+def step_kernel(
+    cache_ref,
+    table_ref,
+    batch_ref,
+    loss_ref,
+    w_ref,
+    head_ref,
+    home_ref,
+    lists_ref,
+    fetch_counts,
+    evict_counts,
+    grad_out,
+    table_out,
+    fetched_out,
+    hot,
+    hot_t,
+    loss_col,
+    base,
+    delta,
+    term,
+    from_core,
+    from_first,
+    from_second,
+    to_z,
+    from_z,
+    whole,
+    slots_out,
+    slots_in,
+    rows_out,
+    evict_out,
+    evict_in,
+    sum_send,
+    sum_recv,
+    row_send,
+    row_recv,
+):
+    group = 4
+    z = lax.axis_index("shard")
+    dp = lax.axis_index("dp")
+    core = dp % 2
+    x = (dp // 2) % 2
+    y = dp // 4
+    by_core = {"dp": dp + 1 - 2 * core}
+    by_x = {"dp": dp + 2 - 4 * x}
+    by_y = {"dp": dp + 4 - 8 * y}
+    near = (by_core, by_x, by_y)
+    along = [{"shard": (z + d) % group} for d in range(1, group)]
+
+    barrier = pltpu.get_barrier_semaphore()
+    for device in near + tuple(along):
+        pl.semaphore_signal(
+            barrier, inc=1, device_id=device, device_id_type=pl.DeviceIdType.MESH
+        )
+
+    samples, features = batch_ref.shape[2], batch_ref.shape[3]
+    cached = cache_ref.shape[2]
+    embed = cache_ref.shape[3] // 3
+    slots = table_ref.shape[2]
+    width = w_ref.shape[1]
+    capacity = fetched_out.shape[3]
+    n_chunks = width // CHUNK
+    columns = features * cached
+
+    pending = []
+
+    def send(src, dst, sends, recvs, at, device):
+        copy = pltpu.make_async_remote_copy(
+            src_ref=src,
+            dst_ref=dst,
+            send_sem=sends.at[at],
+            recv_sem=recvs.at[at],
+            device_id=device,
+            device_id_type=pl.DeviceIdType.MESH,
+        )
+        copy.start()
+        pending.append(copy)
+        return copy
+
+    home = (home_ref[...] % slots).astype(BF)
+    home = jnp.broadcast_to(home.astype(F32), (8, home.shape[1])).astype(BF)
+    listed = lists_ref[...]
+    names = listed[:, : 2 * capacity]
+    row_id = lax.broadcasted_iota(jnp.int32, (home.shape[1], 2 * capacity), 0)
+    lane = lax.broadcasted_iota(jnp.int32, (8, 2 * capacity), 1)
+    for j in range(group):
+        hit = (row_id == names[j : j + 1, :]).astype(F32).astype(BF)
+        found = dot(home, hit, NN).astype(jnp.int32)
+        limit = jnp.where(lane < capacity, fetch_counts[0, 0, j], evict_counts[0, 0, j])
+        found = jnp.where(lane % capacity < limit, found, -1)
+        slots_out[j] = jnp.full(slots_out.shape[1:], -1, jnp.int32)
+        slots_out[j, :, : 2 * capacity] = found
+    slots_in[z] = slots_out[z]
+
+    batch = batch_ref[0, 0].astype(F32).astype(BF)
+    at_f = lax.broadcasted_iota(jnp.int32, (features, columns), 0)
+    at_c = lax.broadcasted_iota(jnp.int32, (features, columns), 1)
+    spread = (at_c // cached == at_f).astype(F32).astype(BF)
+    at_f_t = lax.broadcasted_iota(jnp.int32, (columns, features), 1)
+    at_c_t = lax.broadcasted_iota(jnp.int32, (columns, features), 0)
+    spread_t = (at_c_t // cached == at_f_t).astype(F32).astype(BF)
+    own_c = (lax.broadcasted_iota(jnp.int32, (samples, columns), 1) % cached).astype(F32)
+    hot[...] = (dot(batch, spread, NN) == own_c).astype(F32).astype(BF)
+    own_c_t = (lax.broadcasted_iota(jnp.int32, (columns, samples), 0) % cached).astype(F32)
+    hot_t[...] = (dot(spread_t, batch, NT) == own_c_t).astype(F32).astype(BF)
+    for t in range(samples // 128):
+        piece = loss_ref[0, :, t * 128 : (t + 1) * 128]
+        loss_col[t * 128 : (t + 1) * 128, :] = jnp.broadcast_to(piece, (128, 128)).T
+
+    value = cache_ref[0, 0, :, :embed]
+    value_bf = value.astype(BF)
+    value_t = value.T.astype(BF)
+    value_t2 = jnp.concatenate([value_t, value_t], axis=1)
+
+    pl.semaphore_wait(barrier, len(near) + group - 1)
+    slot_copies = []
+    for d in range(1, group):
+        peer = (z + d) % group
+        slot_copies.append(
+            send(slots_out.at[peer], slots_in.at[z], row_send, row_recv, d - 1, along[d - 1])
+        )
+
+    grads = [jnp.zeros((cached, embed), F32)]
+    copies = {}
+    n_sem = 13
+
+    def compute(k):
+        cols = slice(k * CHUNK, (k + 1) * CHUNK)
+        for f in range(features):
+            part = dot(value_bf, w_ref[f * embed : (f + 1) * embed, cols], NN)
+            high, low = split_two(part)
+            base[0, f * cached : (f + 1) * cached, :] = high
+            base[1, f * cached : (f + 1) * cached, :] = low
+        head = head_ref[:, cols]
+        block = 256
+
+        def rows(t, carry):
+            at = pl.ds(pl.multiple_of(t * block, block), block)
+            pre = dot(hot[at, :], base[0], NN) + dot(hot[at, :], base[1], NN)
+            sigma = 1.0 / (1.0 + jnp.exp(-pre))
+            loss = loss_col[at, :]
+            loss = jnp.concatenate([loss] * (CHUNK // 128), axis=1)
+            delta[at, :] = (loss * head * sigma * (1.0 + pre * (1.0 - sigma))).astype(BF)
+            return carry
+
+        lax.fori_loop(0, samples // block, rows, 0)
+        for f in range(features):
+            summed = dot(hot_t[f * cached : (f + 1) * cached, :], delta[...], NN)
+            high, low = split_two(summed)
+            both = jnp.concatenate([high, low], axis=0)
+            piece = dot(value_t2, both, NN)
+            term[k, f % 2, :, :, :, f // 2] = piece.reshape(2, 2, 2, PIECE, CHUNK)
+            g = dot(both, w_ref[f * embed : (f + 1) * embed, cols], NT)
+            grads[0] = grads[0] + g[:cached] + g[cached:]
+        copies[k, 0] = send(
+            term.at[k, 1 - core], from_core.at[k], sum_send, sum_recv, k * n_sem, by_core
+        )
+
+    def first(k):
+        copies[k, 0].wait_recv()
+        term[k, core] = term[k, core] + from_core[k]
+        copies[k, 1] = send(
+            term.at[k, core, 0, 1 - x], from_first.at[k, 0], sum_send, sum_recv, k * n_sem + 1, by_x
+        )
+        copies[k, 2] = send(
+            term.at[k, core, 1, 1 - y], from_first.at[k, 1], sum_send, sum_recv, k * n_sem + 2, by_y
+        )
+
+    def second(k):
+        copies[k, 1].wait_recv()
+        term[k, core, 0, x] = term[k, core, 0, x] + from_first[k, 0]
+        copies[k, 3] = send(
+            term.at[k, core, 0, x, 1 - y], from_second.at[k, 0], sum_send, sum_recv, k * n_sem + 3, by_y
+        )
+        copies[k, 2].wait_recv()
+        term[k, core, 1, y] = term[k, core, 1, y] + from_first[k, 1]
+        copies[k, 4] = send(
+            term.at[k, core, 1, y, 1 - x], from_second.at[k, 1], sum_send, sum_recv, k * n_sem + 4, by_x
+        )
+
+    def third(k):
+        copies[k, 3].wait_recv()
+        to_z[k, :, 0] = term[k, core, 0, x, y] + from_second[k, 0]
+        copies[k, 4].wait_recv()
+        to_z[k, :, 1] = term[k, core, 1, y, x] + from_second[k, 1]
+        for d in range(1, group):
+            peer = (z + d) % group
+            copies[k, 4 + d] = send(
+                to_z.at[k, peer], from_z.at[k, d - 1], sum_send, sum_recv, k * n_sem + 4 + d, along[d - 1]
+            )
+
+    def fourth(k):
+        for d in range(1, group):
+            copies[k, 4 + d].wait_recv()
+        total = (to_z[k, z] + from_z[k, 0]) + (from_z[k, 1] + from_z[k, 2])
+        whole[k, core, 0, x, y] = total[0]
+        whole[k, core, 1, y, x] = total[1]
+        mine = whole.at[k, core, 0, x, y]
+        copies[k, 8] = send(mine, mine, sum_send, sum_recv, k * n_sem + 8, by_y)
+        mine = whole.at[k, core, 1, y, x]
+        copies[k, 9] = send(mine, mine, sum_send, sum_recv, k * n_sem + 9, by_x)
+
+    def fifth(k):
+        copies[k, 8].wait_recv()
+        mine = whole.at[k, core, 0, x]
+        copies[k, 10] = send(mine, mine, sum_send, sum_recv, k * n_sem + 10, by_x)
+        copies[k, 9].wait_recv()
+        mine = whole.at[k, core, 1, y]
+        copies[k, 11] = send(mine, mine, sum_send, sum_recv, k * n_sem + 11, by_y)
+
+    def sixth(k):
+        copies[k, 10].wait_recv()
+        copies[k, 11].wait_recv()
+        mine = whole.at[k, core]
+        copies[k, 12] = send(mine, mine, sum_send, sum_recv, k * n_sem + 12, by_core)
+
+    scale = 1.0 / math.sqrt(samples * 32)
+
+    def seventh(k):
+        copies[k, 12].wait_recv()
+        got = whole[k].reshape(16 * PIECE, CHUNK)
+        grad_out[:, k * CHUNK : (k + 1) * CHUNK] = (got * scale).astype(BF)
+
+    fetch_copies = []
+    slot_id = lax.broadcasted_iota(jnp.int32, (slots, 2 * capacity), 0)
+    slot_lane = lax.broadcasted_iota(jnp.int32, (slots, 2 * capacity), 1)
+
+    def give():
+        for copy in slot_copies:
+            copy.wait_recv()
+        for i in range(group):
+            hit = (slot_id == slots_in[i, :1, : 2 * capacity]).astype(F32)
+            rows = dot(hit, table_ref[0, 0], TN, EXACT)
+            rows_out[i] = rows[:capacity]
+        fetched_out[0, 0, z] = rows_out[z]
+        for d in range(1, group):
+            peer = (z + d) % group
+            fetch_copies.append(
+                send(rows_out.at[peer], fetched_out.at[0, 0, z], row_send, row_recv, 2 + d, along[d - 1])
+            )
+
+    evict_copies = []
+
+    def write_back():
+        state = cache_ref[0, 0]
+        g = grads[0]
+        moment = beta_one * state[:, embed : 2 * embed] + (1.0 - beta_one) * g
+        second_moment = beta_two * state[:, 2 * embed :] + (1.0 - beta_two) * g * g
+        new = state[:, :embed] - learn_rate * (moment / bias_one) / (
+            jnp.sqrt(second_moment / bias_two) + epsilon
+        )
+        updated = jnp.concatenate([new, moment, second_moment], axis=1)
+        position = lax.broadcasted_iota(jnp.int32, (cached, 3 * capacity), 0)
+        for j in range(group):
+            hit = (position == listed[j : j + 1, :]).astype(F32)
+            rows = dot(hit, updated, TN, EXACT)
+            evict_out[j] = rows[2 * capacity :]
+        evict_in[z] = evict_out[z]
+        for d in range(1, group):
+            peer = (z + d) % group
+            evict_copies.append(
+                send(evict_out.at[peer], evict_in.at[z], row_send, row_recv, 5 + d, along[d - 1])
+            )
+
+    def place():
+        for copy in evict_copies:
+            copy.wait_recv()
+        new = jnp.zeros(table_ref.shape[2:], F32)
+        hits = jnp.zeros((slots, 2 * capacity), F32)
+        for i in range(group):
+            hit = (slot_id == slots_in[i, :1, : 2 * capacity]) & (slot_lane >= capacity)
+            hit = hit.astype(F32)
+            hits = hits + hit
+            rows = jnp.concatenate([jnp.zeros_like(evict_in[i]), evict_in[i]], axis=0)
+            new = new + dot(hit, rows, NN, EXACT)
+        written = jnp.sum(hits, axis=1, keepdims=True) > 0.5
+        table_out[0, 0] = jnp.where(written, new, table_ref[0, 0])
+        for copy in fetch_copies:
+            copy.wait_recv()
+
+    stages = (compute, first, second, third, fourth, fifth, sixth, seventh)
+    for step in range(n_chunks + len(stages) - 1):
+        for s in reversed(range(len(stages))):
+            k = step - s
+            if 0 <= k < n_chunks:
+                stages[s](k)
+        if step == 0:
+            give()
+        if step == n_chunks:
+            write_back()
+        if step == n_chunks + 2:
+            place()
+    for copy in pending:
+        copy.wait_send()
+
+
+def fused(
+    cache_state,
+    table_state,
+    batch_idx,
+    loss_grad,
+    w_first,
+    head,
+    home,
+    fetch_rows,
+    fetch_counts,
+    evict_rows,
+    evict_from,
+    evict_counts,
+):
+    group = lax.axis_size("shard")
+    width = w_first.shape[1]
+    samples, features = batch_idx.shape[2:]
+    cached, state = cache_state.shape[2:]
+    slots = table_state.shape[2]
+    capacity = fetch_rows.shape[3]
+    n_chunks = width // CHUNK
+    lists = jnp.concatenate([fetch_rows[0, 0], evict_rows[0, 0], evict_from[0, 0]], axis=1)
+    columns = features * cached
+    vmem = pl.BlockSpec(memory_space=pltpu.VMEM)
+    smem = pl.BlockSpec(memory_space=pltpu.SMEM)
+    return pl.pallas_call(
+        step_kernel,
+        out_shape=(
+            jax.ShapeDtypeStruct((w_first.shape[0] // group, width), BF),
+            jax.ShapeDtypeStruct(table_state.shape, F32),
+            jax.ShapeDtypeStruct((1, 1, group, capacity, state), F32),
+        ),
+        in_specs=[vmem] * 8 + [smem] * 2,
+        out_specs=(vmem, vmem, vmem),
+        scratch_shapes=[
+            pltpu.VMEM((samples, columns), BF),
+            pltpu.VMEM((columns, samples), BF),
+            pltpu.VMEM((samples, 128), F32),
+            pltpu.VMEM((2, columns, CHUNK), BF),
+            pltpu.VMEM((samples, CHUNK), BF),
+            pltpu.VMEM((n_chunks, 2, 2, 2, 2, group, PIECE, CHUNK), F32),
+            pltpu.VMEM((n_chunks, 2, 2, 2, group, PIECE, CHUNK), F32),
+            pltpu.VMEM((n_chunks, 2, 2, group, PIECE, CHUNK), F32),
+            pltpu.VMEM((n_chunks, 2, group, PIECE, CHUNK), F32),
+            pltpu.VMEM((n_chunks, group, 2, PIECE, CHUNK), F32),
+            pltpu.VMEM((n_chunks, group - 1, 2, PIECE, CHUNK), F32),
+            pltpu.VMEM((n_chunks, 2, 2, 2, 2, PIECE, CHUNK), F32),
+            pltpu.VMEM((group, 8, 128), jnp.int32),
+            pltpu.VMEM((group, 8, 128), jnp.int32),
+            pltpu.VMEM((group, capacity, state), F32),
+            pltpu.VMEM((group, capacity, state), F32),
+            pltpu.VMEM((group, capacity, state), F32),
+            pltpu.SemaphoreType.DMA((n_chunks * 13,)),
+            pltpu.SemaphoreType.DMA((n_chunks * 13,)),
+            pltpu.SemaphoreType.DMA((9,)),
+            pltpu.SemaphoreType.DMA((9,)),
+        ],
+        compiler_params=pltpu.CompilerParams(
+            collective_id=0, has_side_effects=True, vmem_limit_bytes=48 * 1024 * 1024
+        ),
+    )(
+        cache_state,
+        table_state,
+        batch_idx,
+        loss_grad,
+        w_first,
+        head[None, :],
+        home,
+        lists,
+        fetch_counts,
+        evict_counts,
+    )
+
+
 def solution(mesh):
     placed = (
         P("dp", "shard", None, None),
@@ -125,8 +520,9 @@
         P("dp", "shard", None, None),
         P("dp", "shard", None),
     )
+    fits = mesh.shape["shard"] == 4 and mesh.shape["dp"] == 8
     return jax.shard_map(
-        local,
+        fused if fits else local,
         mesh=mesh,
         in_specs=placed,
         out_specs=(

time: 209 us -> 61 us (0.29)
  waiting for transfers between devices: 97.4 us -> 0 us
  Pallas kernels: 0 us -> 49.3 us
  local copies, waits for them, and re-layouts: 51.6 us -> 9.83 us
  matrix products: 19.6 us -> 0 us
  starting transfers between devices: 17.3 us -> 0 us
  between operations: 14.3 us -> 0.66 us
  other arithmetic: 6.55 us -> 0.79 us
    pallas_call x0 -> x1, Pallas kernels: none -> 49.3 us  [fused(): pl.pallas_call(step_kernel, out_shape=(jax.ShapeDtypeStruct((w_first.shap...]
    reduce_scatter x1 -> x0, waiting for transfers between devices: 48.8 us -> none  [local(): lax.psum_scatter(lax.dot_general(inputs, delta, (((0,), (0,)), ((), ())),...]
    psum x1 -> x0, waiting for transfers between devices: 42.2 us -> none  [local(): mine = lax.psum(partial_rows, 'dp')]
    gather x8 -> x0, local copies, waits for them, and re-layouts: 36.6 us -> none  [the longest x2 33.6 us: local(): looked = jnp.take(cache[:, :embed], flat_batch, axis=0)]
    dot_general x4 -> x0, matrix products: 19.6 us -> none  [the longest x1 5.95 us: local(): lax.dot_general(delta, w_first, (((1,), (1,)), ((), ())), preferred_eleme...]
    all_to_all x4 -> x0, starting transfers between devices: 17.3 us -> none  [the longest x1 5.57 us: local(): lax.all_to_all(wanted, 'shard', split_axis=0, concat_axis=0, tiled=True)]
    all_to_all x4 -> x0, waiting for transfers between devices: 6.41 us -> none  [the longest x1 3.7 us: local(): lax.all_to_all(jnp.take(table, place, axis=0), 'shard', split_axis=0, con...]
    unnamed x24 -> x20, local copies, waits for them, and re-layouts: 3.43 us -> 9.83 us
  transfers between devices with their start and end apart: 6 -> 0, of which waited for: 4 -> 0; matrix products, arithmetic and copies ran while one was open for 12% -> 0% of each run, Pallas kernels for 0% -> 0%
where the time goes in v1:
time: 61 us; the launch traced here: 60.6 us
  Pallas kernels  49.3 us (81%)
  local copies, waits for them, and re-layouts  9.83 us (16%)
  other arithmetic  0.79 us (1%)
  between operations  0.66 us (1%)
    pallas_call x1, Pallas kernels, fused(): pl.pallas_call(step_kernel, out_shape=(jax.ShapeDtypeStruct((w_first.shap...  49.3 us
    unnamed x20, local copies, waits for them, and re-layouts  9.83 us

profile of v1, /device:TPU:1, one launch (start us, length us, event | category | flops | bytes accessed | tf_op | source)
XLA Modules:
  0.0 60.6 jit_solution(8344758121758002764)
XLA Ops:
  0.6 0.8 %pad_add_fusion.lists_ref = s32[4,48]{1,0:T(4,128)S(1)} fusion(s32[4,16]{1,0:T(4,128)} %bitcast.5, s32[4,16]{1,0:T(4,128)} %bitcast.6, s32[4,16]{1,0:T(4,128)} %bitcast.7), kind=kLoop, calls=%fused_computation | loop fusion | flops 384 | bytes 1536 | tf_op jit(solution)/shard_map/concatenate | solution.py:455
  1.4 1.0 %copy.15.batch_ref = s32[1,1,1024,8]{3,2,1,0:T(8,128)S(1)} copy(s32[1,1,1024,8]{2,3,1,0:T(8,128)} %param.14) | data formatting | bytes 65536 | tf_op args[2]
  2.4 0.0 copy-start
  2.4 1.6 %copy-done = bf16[1024,1024]{1,0:T(8,128)(2,1)S(1)} copy-done((bf16[1024,1024]{1,0:T(8,128)(2,1)S(1)}, bf16[1024,1024]{1,0:T(8,128)(2,1)}, u32[]{:S(2)}) %copy-start) | copy-done | bytes 2097176
  4.0 0.0 copy-start.1
  4.0 0.9 %copy-done.1 = f32[1,1,128,384]{3,2,1,0:T(8,128)S(1)} copy-done((f32[1,1,128,384]{3,2,1,0:T(8,128)S(1)}, f32[1,1,128,384]{3,2,1,0:T(8,128)}, u32[]{:S(2)}) %copy-start.1) | copy-done | bytes 196632
  4.9 0.0 copy-start.2
  4.9 0.9 %copy-done.2 = f32[1,1,64,384]{3,2,1,0:T(8,128)S(1)} copy-done((f32[1,1,64,384]{3,2,1,0:T(8,128)S(1)}, f32[1,1,64,384]{3,2,1,0:T(8,128)}, u32[]{:S(2)}) %copy-start.2) | copy-done | bytes 98328
  5.8 0.0 copy-start.3
  5.8 0.7 %copy-done.3 = f32[1,1,1024]{2,1,0:T(1,128)S(1)} copy-done((f32[1,1,1024]{2,1,0:T(1,128)S(1)}, f32[1,1,1024]{2,1,0:T(1,128)}, u32[]{:S(2)}) %copy-start.3) | copy-done | bytes 4120
  6.5 0.0 copy-start.4
  6.5 0.7 %copy-done.4 = f32[1024]{0:T(1024)S(1)} copy-done((f32[1024]{0:T(1024)S(1)}, f32[1024]{0:T(1024)}, u32[]{:S(2)}) %copy-start.4) | copy-done | bytes 4120
  7.2 0.0 copy-start.5
  7.2 0.7 %copy-done.5 = s32[1,512]{1,0:T(1,128)S(1)} copy-done((s32[1,512]{1,0:T(1,128)S(1)}, s32[1,512]{1,0:T(1,128)}, u32[]{:S(2)}) %copy-start.5) | copy-done | bytes 2072
  7.9 0.0 copy-start.6
  7.9 0.7 %copy-done.6 = s32[1,1,4]{2,1,0:T(1,128)S(1)} copy-done((s32[1,1,4]{2,1,0:T(1,128)S(1)}, s32[1,1,4]{2,1,0:T(1,128)}, u32[]{:S(2)}) %copy-start.6) | copy-done | bytes 40
  8.5 0.0 copy-start.7
  8.5 0.7 %copy-done.7 = s32[1,1,4]{2,1,0:T(1,128)S(1)} copy-done((s32[1,1,4]{2,1,0:T(1,128)S(1)}, s32[1,1,4]{2,1,0:T(1,128)}, u32[]{:S(2)}) %copy-start.7) | copy-done | bytes 40
  9.2 49.3 %shard_map.139 = (bf16[256,1024]{1,0:T(8,128)(2,1)S(1)}, f32[1,1,128,384]{3,2,1,0:T(8,128)S(1)}, f32[1,1,4,16,384]{4,3,2,1,0:T(8,128)S(1)}) custom-call(f32[1,1,64,384]{3,2,1,0:T(8,128)S(1)} %copy-done.2, f32[1,1,128,384]{3,2,1,0:T(8,128)S(1)} %copy-done.1, s32[1,1,1024,8]{3,2,1,0:T(8,128)S(1)} %copy.15.batch_ref, f32[1,1,1024]{2,1,0:T(1,128)S(1)} %copy-done.3, ...), custom_call_target="tpu_custom_call" | custom-call | tf_op jit(solution)/shard_map/pallas_call | solution.py:459
  58.5 0.8 %copy.19 = bf16[256,1024]{1,0:T(8,128)(2,1)} copy(bf16[256,1024]{1,0:T(8,128)(2,1)S(1)} %get-tuple-element.6) | data formatting | bytes 1048576
  59.3 0.7 %copy.20 = f32[1,1,128,384]{3,2,1,0:T(8,128)} copy(f32[1,1,128,384]{3,2,1,0:T(8,128)S(1)} %get-tuple-element.7) | data formatting | bytes 393216
  59.9 0.6 %copy.21 = f32[1,1,4,16,384]{4,3,2,1,0:T(8,128)} copy(f32[1,1,4,16,384]{4,3,2,1,0:T(8,128)S(1)} %get-tuple-element.8) | data formatting | bytes 196608
Async XLA Ops:
  2.4 1.6 %copy-start = (bf16[1024,1024]{1,0:T(8,128)(2,1)S(1)}, bf16[1024,1024]{1,0:T(8,128)(2,1)}, u32[]{:S(2)}) copy-start(bf16[1024,1024]{1,0:T(8,128)(2,1)} %w_ref.1) | copy-start | bytes 6291460
  4.0 0.9 %copy-start.1 = (f32[1,1,128,384]{3,2,1,0:T(8,128)S(1)}, f32[1,1,128,384]{3,2,1,0:T(8,128)}, u32[]{:S(2)}) copy-start(f32[1,1,128,384]{3,2,1,0:T(8,128)} %table_ref.1) | copy-start | bytes 589828
  4.9 0.9 %copy-start.2 = (f32[1,1,64,384]{3,2,1,0:T(8,128)S(1)}, f32[1,1,64,384]{3,2,1,0:T(8,128)}, u32[]{:S(2)}) copy-start(f32[1,1,64,384]{3,2,1,0:T(8,128)} %cache_ref.1) | copy-start | bytes 294916
  5.8 0.7 %copy-start.3 = (f32[1,1,1024]{2,1,0:T(1,128)S(1)}, f32[1,1,1024]{2,1,0:T(1,128)}, u32[]{:S(2)}) copy-start(f32[1,1,1024]{2,1,0:T(1,128)} %loss_ref.1) | copy-start | bytes 12292
  6.5 0.7 %copy-start.4 = (f32[1024]{0:T(1024)S(1)}, f32[1024]{0:T(1024)}, u32[]{:S(2)}) copy-start(f32[1024]{0:T(1024)} %param.17) | copy-start | bytes 12292
  7.2 0.7 %copy-start.5 = (s32[1,512]{1,0:T(1,128)S(1)}, s32[1,512]{1,0:T(1,128)}, u32[]{:S(2)}) copy-start(s32[1,512]{1,0:T(1,128)} %home_ref.1) | copy-start | bytes 6148
  7.9 0.7 %copy-start.6 = (s32[1,1,4]{2,1,0:T(1,128)S(1)}, s32[1,1,4]{2,1,0:T(1,128)}, u32[]{:S(2)}) copy-start(s32[1,1,4]{2,1,0:T(1,128)} %fetch_counts.1) | copy-start | bytes 52
  8.5 0.7 %copy-start.7 = (s32[1,1,4]{2,1,0:T(1,128)S(1)}, s32[1,1,4]{2,1,0:T(1,128)}, u32[]{:S(2)}) copy-start(s32[1,1,4]{2,1,0:T(1,128)} %evict_counts.1) | copy-start | bytes 52

commit v2 on v1

--- a/solution.py
+++ b/solution.py
@@ -137,14 +137,16 @@
 
 
 def step_kernel(
-    cache_ref,
-    table_ref,
-    batch_ref,
-    loss_ref,
-    w_ref,
-    head_ref,
-    home_ref,
-    lists_ref,
+    cache_hbm,
+    table_hbm,
+    batch_hbm,
+    loss_hbm,
+    w_hbm,
+    head_hbm,
+    home_hbm,
+    fetch_hbm,
+    evict_hbm,
+    source_hbm,
     fetch_counts,
     evict_counts,
     grad_out,
@@ -171,6 +173,18 @@
     sum_recv,
     row_send,
     row_recv,
+    cache_ref,
+    table_ref,
+    batch_ref,
+    loss_ref,
+    w_ref,
+    head_ref,
+    home_ref,
+    fetch_ref,
+    evict_ref,
+    source_ref,
+    load_sem,
+    by_place,
 ):
     group = 4
     z = lax.axis_index("shard")
@@ -190,13 +204,33 @@
             barrier, inc=1, device_id=device, device_id_type=pl.DeviceIdType.MESH
         )
 
-    samples, features = batch_ref.shape[2], batch_ref.shape[3]
+    loads = {}
+    width = w_ref.shape[1]
+    n_chunks = width // CHUNK
+
+    def load(name, src, dst):
+        loads[name] = pltpu.make_async_copy(src, dst, load_sem.at[len(loads)])
+        loads[name].start()
+
+    load("batch", batch_hbm, batch_ref)
+    load("cache", cache_hbm, cache_ref)
+    load("w0", w_hbm.at[:, pl.ds(0, CHUNK)], w_ref.at[:, pl.ds(0, CHUNK)])
+    load("loss", loss_hbm, loss_ref)
+    load("head", head_hbm, head_ref)
+    load("home", home_hbm, home_ref)
+    load("fetch", fetch_hbm, fetch_ref)
+    load("evict", evict_hbm, evict_ref)
+    load("source", source_hbm, source_ref)
+    load("table", table_hbm, table_ref)
+    for k in range(1, n_chunks):
+        cols = pl.ds(k * CHUNK, CHUNK)
+        load(f"w{k}", w_hbm.at[:, cols], w_ref.at[:, cols])
+
+    features, samples = batch_ref.shape[2], batch_ref.shape[3]
     cached = cache_ref.shape[2]
     embed = cache_ref.shape[3] // 3
     slots = table_ref.shape[2]
-    width = w_ref.shape[1]
     capacity = fetched_out.shape[3]
-    n_chunks = width // CHUNK
     columns = features * cached
 
     pending = []
@@ -214,10 +248,32 @@
         pending.append(copy)
         return copy
 
+    loads["batch"].wait()
+    batch = batch_ref[0, 0].astype(F32).astype(BF)
+    at_f = lax.broadcasted_iota(jnp.int32, (features, columns), 0) * cached
+    at_c = lax.broadcasted_iota(jnp.int32, (features, columns), 1)
+    spread = ((at_c >= at_f) & (at_c < at_f + cached)).astype(F32).astype(BF)
+    at_f_t = lax.broadcasted_iota(jnp.int32, (columns, features), 1) * cached
+    at_c_t = lax.broadcasted_iota(jnp.int32, (columns, features), 0)
+    spread_t = ((at_c_t >= at_f_t) & (at_c_t < at_f_t + cached)).astype(F32).astype(BF)
+    own_c = (lax.broadcasted_iota(jnp.int32, (1, columns), 1) % cached).astype(F32)
+    one, zero = jnp.float32(1), jnp.float32(0)
+    hot[...] = jnp.where(dot(batch, spread, TN) == own_c, one, zero).astype(BF)
+    own_c_t = lax.broadcasted_iota(jnp.int32, (cached, samples), 0).astype(F32)
+    for f in range(features):
+        rows = slice(f * cached, (f + 1) * cached)
+        spot = dot(spread_t[rows], batch, NN)
+        hot_t[rows, :] = jnp.where(spot == own_c_t, one, zero).astype(BF)
+    loads["loss"].wait()
+    for t in range(samples // 128):
+        piece = loss_ref[0, :, t * 128 : (t + 1) * 128]
+        loss_col[t * 128 : (t + 1) * 128, :] = jnp.broadcast_to(piece, (128, 128)).T
+
+    for name in ("home", "fetch", "evict", "source"):
+        loads[name].wait()
     home = (home_ref[...] % slots).astype(BF)
     home = jnp.broadcast_to(home.astype(F32), (8, home.shape[1])).astype(BF)
-    listed = lists_ref[...]
-    names = listed[:, : 2 * capacity]
+    names = jnp.concatenate([fetch_ref[0, 0], evict_ref[0, 0]], axis=1)
     row_id = lax.broadcasted_iota(jnp.int32, (home.shape[1], 2 * capacity), 0)
     lane = lax.broadcasted_iota(jnp.int32, (8, 2 * capacity), 1)
     for j in range(group):
@@ -229,21 +285,7 @@
         slots_out[j, :, : 2 * capacity] = found
     slots_in[z] = slots_out[z]
 
-    batch = batch_ref[0, 0].astype(F32).astype(BF)
-    at_f = lax.broadcasted_iota(jnp.int32, (features, columns), 0)
-    at_c = lax.broadcasted_iota(jnp.int32, (features, columns), 1)
-    spread = (at_c // cached == at_f).astype(F32).astype(BF)
-    at_f_t = lax.broadcasted_iota(jnp.int32, (columns, features), 1)
-    at_c_t = lax.broadcasted_iota(jnp.int32, (columns, features), 0)
-    spread_t = (at_c_t // cached == at_f_t).astype(F32).astype(BF)
-    own_c = (lax.broadcasted_iota(jnp.int32, (samples, columns), 1) % cached).astype(F32)
-    hot[...] = (dot(batch, spread, NN) == own_c).astype(F32).astype(BF)
-    own_c_t = (lax.broadcasted_iota(jnp.int32, (columns, samples), 0) % cached).astype(F32)
-    hot_t[...] = (dot(spread_t, batch, NT) == own_c_t).astype(F32).astype(BF)
-    for t in range(samples // 128):
-        piece = loss_ref[0, :, t * 128 : (t + 1) * 128]
-        loss_col[t * 128 : (t + 1) * 128, :] = jnp.broadcast_to(piece, (128, 128)).T
-
+    loads["cache"].wait()
     value = cache_ref[0, 0, :, :embed]
     value_bf = value.astype(BF)
     value_t = value.T.astype(BF)
@@ -261,8 +303,11 @@
     copies = {}
     n_sem = 13
 
-    def compute(k):
+    def forward(k):
         cols = slice(k * CHUNK, (k + 1) * CHUNK)
+        loads[f"w{k}"].wait()
+        if k == 0:
+            loads["head"].wait()
         for f in range(features):
             part = dot(value_bf, w_ref[f * embed : (f + 1) * embed, cols], NN)
             high, low = split_two(part)
@@ -274,16 +319,19 @@
         def rows(t, carry):
             at = pl.ds(pl.multiple_of(t * block, block), block)
             pre = dot(hot[at, :], base[0], NN) + dot(hot[at, :], base[1], NN)
-            sigma = 1.0 / (1.0 + jnp.exp(-pre))
+            sigma = 0.5 * jnp.tanh(0.5 * pre) + 0.5
             loss = loss_col[at, :]
             loss = jnp.concatenate([loss] * (CHUNK // 128), axis=1)
             delta[at, :] = (loss * head * sigma * (1.0 + pre * (1.0 - sigma))).astype(BF)
             return carry
 
         lax.fori_loop(0, samples // block, rows, 0)
+
+    def backward(k):
+        cols = slice(k * CHUNK, (k + 1) * CHUNK)
+        by_place[...] = dot(hot_t[...], delta[...], NN)
         for f in range(features):
-            summed = dot(hot_t[f * cached : (f + 1) * cached, :], delta[...], NN)
-            high, low = split_two(summed)
+            high, low = split_two(by_place[f * cached : (f + 1) * cached, :])
             both = jnp.concatenate([high, low], axis=0)
             piece = dot(value_t2, both, NN)
             term[k, f % 2, :, :, :, f // 2] = piece.reshape(2, 2, 2, PIECE, CHUNK)
@@ -363,6 +411,7 @@
     slot_lane = lax.broadcasted_iota(jnp.int32, (slots, 2 * capacity), 1)
 
     def give():
+        loads["table"].wait()
         for copy in slot_copies:
             copy.wait_recv()
         for i in range(group):
@@ -387,11 +436,12 @@
             jnp.sqrt(second_moment / bias_two) + epsilon
         )
         updated = jnp.concatenate([new, moment, second_moment], axis=1)
-        position = lax.broadcasted_iota(jnp.int32, (cached, 3 * capacity), 0)
+        position = lax.broadcasted_iota(jnp.int32, (cached, capacity), 0)
+        listed = source_ref[0, 0]
         for j in range(group):
             hit = (position == listed[j : j + 1, :]).astype(F32)
             rows = dot(hit, updated, TN, EXACT)
-            evict_out[j] = rows[2 * capacity :]
+            evict_out[j] = rows
         evict_in[z] = evict_out[z]
         for d in range(1, group):
             peer = (z + d) % group
@@ -415,12 +465,16 @@
         for copy in fetch_copies:
             copy.wait_recv()
 
-    stages = (compute, first, second, third, fourth, fifth, sixth, seventh)
-    for step in range(n_chunks + len(stages) - 1):
-        for s in reversed(range(len(stages))):
-            k = step - s
+    later = (first, second, third, fourth, fifth, sixth, seventh)
+    for step in range(n_chunks + len(later)):
+        if step < n_chunks:
+            forward(step)
+        for s, stage in enumerate(later):
+            k = step - 1 - s
             if 0 <= k < n_chunks:
-                stages[s](k)
+                stage(k)
+        if step < n_chunks:
+            backward(step)
         if step == 0:
             give()
         if step == n_chunks:
@@ -452,7 +506,7 @@
     slots = table_state.shape[2]
     capacity = fetch_rows.shape[3]
     n_chunks = width // CHUNK
-    lists = jnp.concatenate([fetch_rows[0, 0], evict_rows[0, 0], evict_from[0, 0]], axis=1)
+    hbm = pl.BlockSpec(memory_space=pl.ANY)
     columns = features * cached
     vmem = pl.BlockSpec(memory_space=pltpu.VMEM)
     smem = pl.BlockSpec(memory_space=pltpu.SMEM)
@@ -463,7 +517,7 @@
             jax.ShapeDtypeStruct(table_state.shape, F32),
             jax.ShapeDtypeStruct((1, 1, group, capacity, state), F32),
         ),
-        in_specs=[vmem] * 8 + [smem] * 2,
+        in_specs=[hbm] * 10 + [smem] * 2,
         out_specs=(vmem, vmem, vmem),
         scratch_shapes=[
             pltpu.VMEM((samples, columns), BF),
@@ -487,19 +541,33 @@
             pltpu.SemaphoreType.DMA((n_chunks * 13,)),
             pltpu.SemaphoreType.DMA((9,)),
             pltpu.SemaphoreType.DMA((9,)),
+            pltpu.VMEM(cache_state.shape, F32),
+            pltpu.VMEM(table_state.shape, F32),
+            pltpu.VMEM((1, 1, features, samples), jnp.int32),
+            pltpu.VMEM(loss_grad.shape, F32),
+            pltpu.VMEM(w_first.shape, BF),
+            pltpu.VMEM((1, width), F32),
+            pltpu.VMEM(home.shape, jnp.int32),
+            pltpu.VMEM(fetch_rows.shape, jnp.int32),
+            pltpu.VMEM(evict_rows.shape, jnp.int32),
+            pltpu.VMEM(evict_from.shape, jnp.int32),
+            pltpu.SemaphoreType.DMA((9 + n_chunks,)),
+            pltpu.VMEM((columns, CHUNK), F32),
         ],
         compiler_params=pltpu.CompilerParams(
-            collective_id=0, has_side_effects=True, vmem_limit_bytes=48 * 1024 * 1024
+            collective_id=0, has_side_effects=True, vmem_limit_bytes=56 * 1024 * 1024
         ),
     )(
         cache_state,
         table_state,
-        batch_idx,
+        jnp.swapaxes(batch_idx, 2, 3),
         loss_grad,
         w_first,
         head[None, :],
         home,
-        lists,
+        fetch_rows,
+        evict_rows,
+        evict_from,
         fetch_counts,
         evict_counts,
     )

time: 61 us -> 52.7 us (0.86)
  local copies, waits for them, and re-layouts: 9.83 us -> 5.02 us
  Pallas kernels: 49.3 us -> 46.8 us
  other arithmetic: 0.79 us -> 0 us
    unnamed x20 -> x3, local copies, waits for them, and re-layouts: 9.83 us -> 5.02 us
    pallas_call x1, Pallas kernels: 49.3 us -> 46.8 us  [fused(): pl.pallas_call(step_kernel, out_shape=(jax.ShapeDtypeStruct((w_first.shap...]
    concatenate x1 -> x0, other arithmetic: 0.79 us -> none  [fused(): jnp.concatenate([fetch_rows[0, 0], evict_rows[0, 0], evict_from[0, 0]], a...]
where the time goes in v2:
time: 52.7 us; the launch traced here: 52.5 us
  Pallas kernels  46.8 us (89%)
  local copies, waits for them, and re-layouts  5.02 us (10%)
  between operations  0.64 us (1%)
    pallas_call x1, Pallas kernels, fused(): pl.pallas_call(step_kernel, out_shape=(jax.ShapeDtypeStruct((w_first.shap...  46.8 us
    unnamed x3, local copies, waits for them, and re-layouts  5.02 us

profile of v2, /device:TPU:1, one launch (start us, length us, event | category | flops | bytes accessed | tf_op | source)
XLA Modules:
  0.0 52.5 jit_solution(8704043140884548861)
XLA Ops:
  0.6 46.8 %shard_map.139 = (bf16[256,1024]{1,0:T(8,128)(2,1)}, f32[1,1,128,384]{3,2,1,0:T(8,128)}, f32[1,1,4,16,384]{4,3,2,1,0:T(8,128)}) custom-call(f32[1,1,64,384]{3,2,1,0:T(8,128)} %cache_hbm.1, f32[1,1,128,384]{3,2,1,0:T(8,128)} %table_hbm.1, s32[1,1,8,1024]{3,2,1,0:T(8,128)} %bitcast.2, f32[1,1,1024]{2,1,0:T(1,128)} %loss_hbm.1, bf16[1024,1024]{1,0:T(8,128)(2,1)} %w_hbm.1, ...), custom_call_target="tpu_custom_call" | custom-call | tf_op jit(solution)/shard_map/pallas_call | solution.py:513
  47.4 1.9 %copy.18 = bf16[256,1024]{1,0:T(8,128)(2,1)} copy(bf16[256,1024]{1,0:T(8,128)(2,1)} %get-tuple-element.6) | data formatting | bytes 1048576
  49.3 1.6 %copy.19 = f32[1,1,128,384]{3,2,1,0:T(8,128)} copy(f32[1,1,128,384]{3,2,1,0:T(8,128)} %get-tuple-element.7) | data formatting | bytes 393216
  50.9 1.5 %copy.20 = f32[1,1,4,16,384]{4,3,2,1,0:T(8,128)} copy(f32[1,1,4,16,384]{4,3,2,1,0:T(8,128)} %get-tuple-element.8) | data formatting | bytes 196608

commit v3 on v2

--- a/solution.py
+++ b/solution.py
@@ -195,7 +195,8 @@
     by_core = {"dp": dp + 1 - 2 * core}
     by_x = {"dp": dp + 2 - 4 * x}
     by_y = {"dp": dp + 4 - 8 * y}
-    near = (by_core, by_x, by_y)
+    by_both = {"dp": dp + 6 - 4 * x - 8 * y}
+    near = (by_core, by_x, by_y, by_both)
     along = [{"shard": (z + d) % group} for d in range(1, group)]
 
     barrier = pltpu.get_barrier_semaphore()
@@ -301,7 +302,7 @@
 
     grads = [jnp.zeros((cached, embed), F32)]
     copies = {}
-    n_sem = 13
+    n_sem = 15
 
     def forward(k):
         cols = slice(k * CHUNK, (k + 1) * CHUNK)
@@ -380,29 +381,24 @@
         total = (to_z[k, z] + from_z[k, 0]) + (from_z[k, 1] + from_z[k, 2])
         whole[k, core, 0, x, y] = total[0]
         whole[k, core, 1, y, x] = total[1]
-        mine = whole.at[k, core, 0, x, y]
-        copies[k, 8] = send(mine, mine, sum_send, sum_recv, k * n_sem + 8, by_y)
-        mine = whole.at[k, core, 1, y, x]
-        copies[k, 9] = send(mine, mine, sum_send, sum_recv, k * n_sem + 9, by_x)
+        at = 8
+        for mine in (whole.at[k, core, 0, x, y], whole.at[k, core, 1, y, x]):
+            for device in (by_both, by_x, by_y):
+                copies[k, at] = send(
+                    mine, mine, sum_send, sum_recv, k * n_sem + at, device
+                )
+                at += 1
 
     def fifth(k):
-        copies[k, 8].wait_recv()
-        mine = whole.at[k, core, 0, x]
-        copies[k, 10] = send(mine, mine, sum_send, sum_recv, k * n_sem + 10, by_x)
-        copies[k, 9].wait_recv()
-        mine = whole.at[k, core, 1, y]
-        copies[k, 11] = send(mine, mine, sum_send, sum_recv, k * n_sem + 11, by_y)
+        for at in range(8, 14):
+            copies[k, at].wait_recv()
+        mine = whole.at[k, core]
+        copies[k, 14] = send(mine, mine, sum_send, sum_recv, k * n_sem + 14, by_core)
+
+    scale = 1.0 / math.sqrt(samples * 32)
 
     def sixth(k):
-        copies[k, 10].wait_recv()
-        copies[k, 11].wait_recv()
-        mine = whole.at[k, core]
-        copies[k, 12] = send(mine, mine, sum_send, sum_recv, k * n_sem + 12, by_core)
-
-    scale = 1.0 / math.sqrt(samples * 32)
-
-    def seventh(k):
-        copies[k, 12].wait_recv()
+        copies[k, 14].wait_recv()
         got = whole[k].reshape(16 * PIECE, CHUNK)
         grad_out[:, k * CHUNK : (k + 1) * CHUNK] = (got * scale).astype(BF)
 
@@ -465,7 +461,7 @@
         for copy in fetch_copies:
             copy.wait_recv()
 
-    later = (first, second, third, fourth, fifth, sixth, seventh)
+    later = (first, second, third, fourth, fifth, sixth)
     for step in range(n_chunks + len(later)):
         if step < n_chunks:
             forward(step)
@@ -475,11 +471,11 @@
                 stage(k)
         if step < n_chunks:
             backward(step)
-        if step == 0:
-            give()
         if step == n_chunks:
             write_back()
-        if step == n_chunks + 2:
+        if step == n_chunks + 1:
+            give()
+        if step == n_chunks + 3:
             place()
     for copy in pending:
         copy.wait_send()
@@ -537,8 +533,8 @@
             pltpu.VMEM((group, capacity, state), F32),
             pltpu.VMEM((group, capacity, state), F32),
             pltpu.VMEM((group, capacity, state), F32),
-            pltpu.SemaphoreType.DMA((n_chunks * 13,)),
-            pltpu.SemaphoreType.DMA((n_chunks * 13,)),
+            pltpu.SemaphoreType.DMA((n_chunks * 15,)),
+            pltpu.SemaphoreType.DMA((n_chunks * 15,)),
             pltpu.SemaphoreType.DMA((9,)),
             pltpu.SemaphoreType.DMA((9,)),
             pltpu.VMEM(cache_state.shape, F32),

time: 52.7 us -> 52.1 us (0.989)
  Pallas kernels: 46.8 us -> 46.2 us
    pallas_call x1, Pallas kernels: 46.8 us -> 46.2 us  [fused(): pl.pallas_call(step_kernel, out_shape=(jax.ShapeDtypeStruct((w_first.shap...]
where the time goes in v3:
time: 52.1 us; the launch traced here: 51.8 us
  Pallas kernels  46.2 us (89%)
  local copies, waits for them, and re-layouts  5.02 us (10%)
  between operations  0.64 us (1%)
    pallas_call x1, Pallas kernels, fused(): pl.pallas_call(step_kernel, out_shape=(jax.ShapeDtypeStruct((w_first.shap...  46.2 us
    unnamed x3, local copies, waits for them, and re-layouts  5.02 us

profile of v3, /device:TPU:1, one launch (start us, length us, event | category | flops | bytes accessed | tf_op | source)
XLA Modules:
  0.0 51.8 jit_solution(14180149687332405876)
XLA Ops:
  0.6 46.2 %shard_map.139 = (bf16[256,1024]{1,0:T(8,128)(2,1)}, f32[1,1,128,384]{3,2,1,0:T(8,128)}, f32[1,1,4,16,384]{4,3,2,1,0:T(8,128)}) custom-call(f32[1,1,64,384]{3,2,1,0:T(8,128)} %cache_hbm.1, f32[1,1,128,384]{3,2,1,0:T(8,128)} %table_hbm.1, s32[1,1,8,1024]{3,2,1,0:T(8,128)} %bitcast.2, f32[1,1,1024]{2,1,0:T(1,128)} %loss_hbm.1, bf16[1024,1024]{1,0:T(8,128)(2,1)} %w_hbm.1, ...), custom_call_target="tpu_custom_call" | custom-call | tf_op jit(solution)/shard_map/pallas_call | solution.py:509
  46.8 1.9 %copy.18 = bf16[256,1024]{1,0:T(8,128)(2,1)} copy(bf16[256,1024]{1,0:T(8,128)(2,1)} %get-tuple-element.6) | data formatting | bytes 1048576
  48.7 1.6 %copy.19 = f32[1,1,128,384]{3,2,1,0:T(8,128)} copy(f32[1,1,128,384]{3,2,1,0:T(8,128)} %get-tuple-element.7) | data formatting | bytes 393216
  50.3 1.5 %copy.20 = f32[1,1,4,16,384]{4,3,2,1,0:T(8,128)} copy(f32[1,1,4,16,384]{4,3,2,1,0:T(8,128)} %get-tuple-element.8) | data formatting | bytes 196608
